TPU v7x, 32 devices: a whole 2x2x4 slice. The times are simulated.
32 devices in a mesh: row: 8 (over y, x, core), col: 4 (over z).
Axes of the slice: x: 2, y: 2, z: 4, core: 2. Of those that a mesh axis runs over, the one named last changes fastest.
Arguments:
- row_emb: float32 [32, 300, 1024], P(('row', 'col')), may hold values from -1.5 to 1.5
- col_emb: float32 [32, 300, 1024], P(('row', 'col')), may hold values from -1.5 to 1.5
- row_acc: float32 [32, 300, 1024], P(('row', 'col')), may hold values from 0.5 to 8
- col_acc: float32 [32, 300, 1024], P(('row', 'col')), may hold values from 0.5 to 8
- marginal_log: float32 [32768], replicated, may hold values from -2 to 1
- tile_rows: int32 [96], P(('row', 'col')), may hold values from 0 to 31, as said below
- tile_cols: int32 [96], P(('row', 'col')), may hold values from 0 to 31, as said below
- counts: int32 [96, 1024, 1024], P(('row', 'col')), may hold values from 0 to 2047
Outputs:
- new_row_emb: float32 [32, 300, 1024], P(('row', 'col'))
- new_col_emb: float32 [32, 300, 1024], P(('row', 'col'))
- new_row_acc: float32 [32, 300, 1024], P(('row', 'col'))
- new_col_acc: float32 [32, 300, 1024], P(('row', 'col'))
Inputs may be any that keep to these rules, and one draw needn't show every extreme that they name: Block g of the embeddings lies on device g in the mesh's order (row slowest). Slot k lies on device p = k // 3; with p at row index r and col index c, tile_rows[k] // 4 equals r. With slot k on the device at col index c, tile_cols[k] % 4 equals c.
All inputs are finite; a program needn't handle non-finite values.
Results may differ from a plain program's by a relative error of at most 0.019.
Values may be sent and summed in bfloat16 or wider, within the bound.
A program may use at most 128 MiB of HBM per device.

v0:
```python
import jax
import jax.numpy as jnp
from jax import lax
from jax.sharding import PartitionSpec as P

err_scale = 0.03125
learn_rate = 0.1


def tile_terms(row_block, col_block, tile_counts, row_margin, col_margin):
    scores = lax.dot_general(
        row_block, col_block, (((0,), (0,)), ((), ())), preferred_element_type=jnp.float32
    )
    counted = tile_counts.astype(jnp.float32)
    shifted_log = jnp.log(jnp.maximum(counted, 1.0)) - row_margin[:, None] - col_margin[None, :]
    residue = scores - shifted_log
    weighted = (0.1 + 0.25 * jnp.sqrt(counted)) * residue
    cell_grad = jnp.where(tile_counts > 0, weighted, jax.nn.sigmoid(residue)) * err_scale
    errors = cell_grad.astype(jnp.bfloat16)
    row_term = lax.dot_general(
        col_block, errors, (((1,), (1,)), ((), ())), preferred_element_type=jnp.float32
    )
    col_term = jnp.dot(row_block, errors, preferred_element_type=jnp.float32)
    return (row_term, col_term)


def add_slot(buffer, slot_index, term):
    old_value = lax.dynamic_index_in_dim(buffer, slot_index, 0, keepdims=False)
    return lax.dynamic_update_index_in_dim(buffer, old_value + term, slot_index, 0)


def adagrad(weights, history, gradient):
    grown = history + gradient * gradient
    return (weights - learn_rate * gradient / jnp.sqrt(grown), grown)


def body(row_emb, col_emb, row_acc, col_acc, marginal_log, tile_rows, tile_cols, counts):
    col_count = lax.axis_size("col")
    row_count = lax.axis_size("row")
    emb_width = row_emb.shape[1]
    block_len = row_emb.shape[2]
    tile_total = counts.shape[0]
    row_low = row_emb.astype(jnp.bfloat16)
    col_low = col_emb.astype(jnp.bfloat16)
    rows_near = lax.all_gather(row_low, "col", axis=0, tiled=True)
    grads = (
        jnp.zeros((col_count, emb_width, block_len), jnp.float32),
        jnp.zeros((row_count, emb_width, block_len), jnp.float32),
    )
    cols_near = lax.all_gather(col_low, "row", axis=0, tiled=True)
    for tile_slot in range(tile_total):
        col_slot = tile_cols[tile_slot] // col_count
        col_block = lax.dynamic_index_in_dim(cols_near, col_slot, 0, keepdims=False)
        row_id = tile_rows[tile_slot]
        col_id = tile_cols[tile_slot]
        row_slot = row_id % col_count
        apply_col_slot = col_id // col_count
        row_block = lax.dynamic_index_in_dim(rows_near, row_slot, 0, keepdims=False)
        row_margin = lax.dynamic_slice_in_dim(marginal_log, row_id * block_len, block_len)
        col_margin = lax.dynamic_slice_in_dim(marginal_log, col_id * block_len, block_len)
        row_term, col_term = tile_terms(
            row_block, col_block, counts[tile_slot], row_margin, col_margin
        )
        grads = (
            add_slot(grads[0], row_slot, row_term),
            add_slot(grads[1], apply_col_slot, col_term),
        )
    row_sum = lax.psum_scatter(
        grads[0].astype(jnp.bfloat16), "col", scatter_dimension=0, tiled=True
    ).astype(jnp.float32)
    col_sum = lax.psum_scatter(
        grads[1].astype(jnp.bfloat16), "row", scatter_dimension=0, tiled=True
    ).astype(jnp.float32)
    new_row_emb, new_row_acc = adagrad(row_emb, row_acc, row_sum)
    new_col_emb, new_col_acc = adagrad(col_emb, col_acc, col_sum)
    return (new_row_emb, new_col_emb, new_row_acc, new_col_acc)


def solution(mesh):
    placed = (
        P(("row", "col"), None, None),
        P(("row", "col"), None, None),
        P(("row", "col"), None, None),
        P(("row", "col"), None, None),
        P(),
        P(("row", "col")),
        P(("row", "col")),
        P(("row", "col"), None, None),
    )
    return jax.shard_map(
        body,
        mesh=mesh,
        in_specs=placed,
        out_specs=(
            P(("row", "col"), None, None),
            P(("row", "col"), None, None),
            P(("row", "col"), None, None),
            P(("row", "col"), None, None),
        ),
        check_vma=False,
    )
```

profile of v0, /device:TPU:9, one launch (start us, length us, event | category | flops | bytes accessed | tf_op | source)
XLA Modules:
  0.0 254.7 jit_solution(11485238663482199903)
XLA Ops:
  7.2 2.3 copy.34
  9.6 2.3 copy.35
  12.0 0.6 fusion.68
  20.4 0.6 fusion.67
  30.7 0.8 fusion.66
  31.5 30.6 %all-gather.5.cloned.1.call-done = bf16[4,300,1024]{2,1,0:T(8,128)(2,1)} async-done(((bf16[1,300,1024]{2,1,0:T(8,128)(2,1)}), bf16[4,300,1024]{2,1,0:T(8,128)(2,1)}) %all-gather.5.cloned.1.call-update) | async-done | bytes 2457616 | tf_op jit(solution)/shard_map/all_gather | solution.py:45
  62.1 43.6 %all-gather.3.cloned.1.call-done = bf16[8,300,1024]{2,1,0:T(8,128)(2,1)} async-done(((bf16[1,300,1024]{2,1,0:T(8,128)(2,1)}), bf16[8,300,1024]{2,1,0:T(8,128)(2,1)}) %all-gather.3.cloned.1.call-update) | async-done | bytes 4915216 | tf_op jit(solution)/shard_map/all_gather | solution.py:50
  105.7 6.7 %fusion.14 = bf16[1024,1024]{1,0:T(8,128)(2,1)S(1)} fusion(s32[3,1024,1024]{2,1,0:T(8,128)} %param.15, f32[1024]{0:T(1024)S(1)} %get-tuple-element.15, f32[1024]{0:T(1024)S(1)} %get-tuple-element.16, bf16[4,300,1024]{2,1,0:T(8,128)(2,1)} %all-gather.5.cloned.1.call-done, s32[]{:T(128)S(6)} %select_n.95, ...), kind=kOutput, calls=%fused_computation.20 | convolution fusion | flops 644874240 | bytes 7544840 | tf_op jit(solution)/shard_map/dot_general | solution.py:11
  113.1 0.8 copy-done.10
  113.8 1.8 copy-done.5
  115.6 0.8 fusion.24
  116.6 0.7 copy-done.8
  117.3 5.8 %fusion.9 = bf16[1024,1024]{1,0:T(8,128)(2,1)S(1)} fusion(s32[3,1024,1024]{2,1,0:T(8,128)} %param.15, f32[1024]{0:T(1024)S(1)} %get-tuple-element.13, f32[1024]{0:T(1024)S(1)} %get-tuple-element.14, bf16[4,300,1024]{2,1,0:T(8,128)(2,1)S(1)} %copy-done.8, s32[]{:T(128)S(6)} %select_n.100, bf16[8,300,1024]{2,1,0:T(8,128)(2,1)S(1)} %copy-done.5, s32[]{:T(128)S(6)} %select_n.102), kind=kOutput, calls=%fused_computation.13 | convolution fusion | flops 644874240 | bytes 7544840 | tf_op jit(solution)/shard_map/dot_general | solution.py:11
  123.1 0.9 fusion.22
  124.1 5.8 %fusion.4 = bf16[1024,1024]{1,0:T(8,128)(2,1)S(1)} fusion(s32[3,1024,1024]{2,1,0:T(8,128)} %param.15, f32[1024]{0:T(1024)S(1)} %get-tuple-element.17, f32[1024]{0:T(1024)S(1)} %get-tuple-element.12, bf16[4,300,1024]{2,1,0:T(8,128)(2,1)S(1)} %copy-done.8, s32[]{:T(128)S(6)} %select_n.107, bf16[8,300,1024]{2,1,0:T(8,128)(2,1)S(1)} %copy-done.5, s32[]{:T(128)S(6)} %select_n.109), kind=kOutput, calls=%fused_computation.6 | convolution fusion | flops 644874240 | bytes 7544840 | tf_op jit(solution)/shard_map/dot_general | solution.py:11
  129.9 1.3 copy-done.2
  131.2 0.9 fusion.20
  132.0 1.9 convert_element_type.47
  134.1 1.3 broadcast_in_dim.36
  135.8 0.6 copy-done.11
  136.5 0.8 fusion.23
  137.4 0.8 fusion.18
  139.0 0.8 fusion.16
  139.8 3.1 %convert_element_type.49 = bf16[8,300,1024]{2,1,0:T(8,128)(2,1)} convert(f32[8,300,1024]{2,1,0:T(8,128)S(1)} %fusion.16) | non-fusion elementwise | flops 2457600 | bytes 14745600 | tf_op jit(solution)/shard_map/convert_element_type | solution.py:72
  142.9 38.5 %reduce-scatter.3.cloned.1.call-done = bf16[1,300,1024]{2,1,0:T(8,128)(2,1)} async-done(((bf16[4,300,1024]{2,1,0:T(8,128)(2,1)}), bf16[1,300,1024]{2,1,0:T(8,128)(2,1)}) %reduce-scatter.3.cloned.1.call-update) | async-done | bytes 614416 | tf_op jit(solution)/shard_map/reduce_scatter | solution.py:68
  181.4 2.2 fusion.26
  183.6 2.3 copy.24
  185.9 2.3 copy.26
  188.2 53.7 %reduce-scatter.5.cloned.1.call-done = bf16[1,300,1024]{2,1,0:T(8,128)(2,1)} async-done(((bf16[8,300,1024]{2,1,0:T(8,128)(2,1)}), bf16[1,300,1024]{2,1,0:T(8,128)(2,1)}) %reduce-scatter.5.cloned.1.call-update) | async-done | bytes 614416 | tf_op jit(solution)/shard_map/reduce_scatter | solution.py:71
  241.9 1.8 fusion.29
  243.6 2.3 copy.25
  245.9 2.3 copy.27
  (32 shorter events, 2.5 us)
Async XLA Ops:
  7.2 4.8 %copy-start.6 = (s32[3]{0:T(128)S(1)}, s32[3]{0:T(128)}, u32[]{:S(2)}) copy-start(s32[3]{0:T(128)} %param.13) | copy-start | bytes 40
  7.2 13.2 %copy-start.7 = (s32[3]{0:T(128)S(1)}, s32[3]{0:T(128)}, u32[]{:S(2)}) copy-start(s32[3]{0:T(128)} %param.14) | copy-start | bytes 40
  7.2 54.9 %all-gather.5.cloned.1.call-start = ((), (), s32[]{:S(2)}) async-start(), calls=%async_computation.3 | async-start | bytes 3112960 | tf_op jit(solution)/shard_map/all_gather | solution.py:45
  9.6 96.2 %all-gather.3.cloned.1.call-start = ((), (), s32[]{:S(2)}) async-start(), calls=%async_computation.2 | async-start | bytes 5603328 | tf_op jit(solution)/shard_map/all_gather | solution.py:50
  11.9 169.5 %reduce-scatter.3.cloned.1.call-start = ((), (), s32[]{:S(2)}) async-start(), calls=%async_computation.4 | async-start | bytes 3112960 | tf_op jit(solution)/shard_map/reduce_scatter | solution.py:68
  112.4 1.4 copy-start.10
  112.4 3.2 %copy-start.5 = (bf16[8,300,1024]{2,1,0:T(8,128)(2,1)S(1)}, bf16[8,300,1024]{2,1,0:T(8,128)(2,1)}, u32[]{:S(2)}) copy-start(bf16[8,300,1024]{2,1,0:T(8,128)(2,1)} %all-gather.3.cloned.1.call-done) | copy-start | bytes 14745604
  115.6 1.7 copy-start.8
  129.8 1.3 copy-start.2
  133.9 108.0 %reduce-scatter.5.cloned.1.call-start = ((), (), s32[]{:S(2)}) async-start(), calls=%async_computation.5 | async-start | bytes 5603328 | tf_op jit(solution)/shard_map/reduce_scatter | solution.py:71
  134.1 1.7 copy-start.9
  134.1 2.3 copy-start.11
  137.4 1.6 copy-start.3
  142.9 38.5 %copy-start = (f32[1,300,1024]{2,0,1:T(1,128)S(1)}, f32[1,300,1024]{2,0,1:T(1,128)}, u32[]{:S(2)}) copy-start(f32[1,300,1024]{2,0,1:T(1,128)} %param.8) | copy-start | bytes 3686404
  142.9 98.9 %copy-start.1 = (f32[1,300,1024]{2,0,1:T(1,128)S(1)}, f32[1,300,1024]{2,0,1:T(1,128)}, u32[]{:S(2)}) copy-start(f32[1,300,1024]{2,0,1:T(1,128)} %param.9) | copy-start | bytes 3686404
  183.6 58.3 %copy-start.4 = (f32[1,300,1024]{2,0,1:T(1,128)S(1)}, f32[1,300,1024]{2,0,1:T(1,128)}, u32[]{:S(2)}) copy-start(f32[1,300,1024]{2,0,1:T(1,128)} %param.11) | copy-start | bytes 3686404
Sparse Core Ops, SparseCore 0:
  10.2 51.9 all-gather.4
  64.6 41.1 all-gather.2
  134.0 47.3 reduce-scatter.2
  184.8 57.0 reduce-scatter.4
where the time goes:
time: 257 us; the launch traced here: 255 us
  waiting for transfers between devices  166 us (65%)
  between operations  31.4 us (12%)
  local copies, waits for them, and re-layouts  24.4 us (9%)
  matrix products  23.3 us (9%)
  other arithmetic  8.85 us (3%)
    reduce_scatter x1, waiting for transfers between devices, body(): lax.psum_scatter(grads[1].astype(jnp.bfloat16), 'row', scatter_dimension=...  53.7 us
    all_gather x1, waiting for transfers between devices, body(): cols_near = lax.all_gather(col_low, 'row', axis=0, tiled=True)  43.6 us
    reduce_scatter x1, waiting for transfers between devices, body(): lax.psum_scatter(grads[0].astype(jnp.bfloat16), 'col', scatter_dimension=...  38.5 us
    all_gather x1, waiting for transfers between devices, body(): rows_near = lax.all_gather(row_low, 'col', axis=0, tiled=True)  30.6 us
    unnamed x30, local copies, waits for them, and re-layouts  20.1 us
    dot_general x3, matrix products, tile_terms(): lax.dot_general(row_block, col_block, (((0,), (0,)), ((), ())), preferred...  18.2 us
  transfers between devices with their start and end apart: 4, of which 4 were waited for; matrix products, arithmetic and copies ran while one was open for 7% of the time, Pallas kernels for 0%

commit v1 on v0

v1 whole, which is shorter than its diff:
```python
import functools

import jax
import jax.numpy as jnp
from jax import lax
from jax.experimental import pallas as pl
from jax.experimental.pallas import tpu as pltpu
from jax.sharding import PartitionSpec as P

err_scale = 0.03125
learn_rate = 0.1
chunk_count = 4
count_slots = 4
MESH = pl.DeviceIdType.MESH


def flip(index, mask):
    bit = 1
    while bit <= mask:
        if mask & bit:
            index = index + bit * (1 - 2 * ((index // bit) % 2))
        bit *= 2
    return index


def step_kernel(n_row, n_col, tiles, row_slots, col_slots, row_pick, col_pick, row_in, col_in,
                counts, row_out, col_out, *scratch):
    nc = chunk_count
    rows_near = scratch[:nc]
    row_send = scratch[nc:2 * nc]
    row_recv = scratch[2 * nc:3 * nc]
    (cols_near, col_part, sib_recv, peer_recv, count_buf, row_term, col_term,
     z_send, z_recv, c_send, c_recv, s_send, s_recv, cnt_sem, rs_send, rs_recv,
     q_send, q_recv, p_send, p_recv) = scratch[3 * nc:]
    chips = n_row // 2
    block_len = row_in.shape[1]
    width = block_len // nc
    r = lax.axis_index("row")
    i = lax.axis_index("col")
    q = r // 2
    core = r % 2
    sib = flip(r, 1)
    has_left = i > 0
    has_right = i < n_col - 1

    def row_dev(index):
        return (index, i)

    def col_dev(index):
        return (r, index)

    def count_copy(piece):
        c, t = piece // tiles, piece % tiles
        return pltpu.make_async_copy(
            counts.at[t, pl.ds(pl.multiple_of(c * width, width), width), :],
            count_buf.at[piece % count_slots], cnt_sem.at[piece % count_slots])

    for piece in range(count_slots):
        count_copy(piece).start()

    for c in range(nc):
        rows_near[c][i] = row_in[:, c * width:(c + 1) * width]
    cols_near[r] = col_in[...]

    barrier = pltpu.get_barrier_semaphore()
    for m in range(1, chips):
        pl.semaphore_signal(barrier, inc=1, device_id=row_dev(2 * flip(q, m) + core), device_id_type=MESH)
    pl.semaphore_signal(barrier, inc=1, device_id=row_dev(sib), device_id_type=MESH)

    @pl.when(has_left)
    def _():
        pl.semaphore_signal(barrier, inc=1, device_id=col_dev(i - 1), device_id_type=MESH)

    @pl.when(has_right)
    def _():
        pl.semaphore_signal(barrier, inc=1, device_id=col_dev(i + 1), device_id_type=MESH)

    pl.semaphore_wait(barrier, chips + jnp.minimum(i, 1) + jnp.minimum(n_col - 1 - i, 1))

    def z_copy(c, block, way):
        return pltpu.make_async_remote_copy(
            src_ref=rows_near[c].at[block], dst_ref=rows_near[c].at[block],
            send_sem=z_send.at[way, c, block], recv_sem=z_recv.at[c, block],
            device_id=col_dev(i + 1 - 2 * way), device_id_type=MESH)

    def z_own(c):
        @pl.when(has_right)
        def _():
            z_copy(c, i, 0).start()

        @pl.when(has_left)
        def _():
            z_copy(c, i, 1).start()

    def z_forward(c):
        for s in range(1, n_col):
            @pl.when(i - s >= 0)
            def _():
                z_copy(c, i - s, 0).wait_recv()

                @pl.when(has_right)
                def _():
                    z_copy(c, i - s, 0).start()

            @pl.when(i + s < n_col)
            def _():
                z_copy(c, i + s, 1).wait_recv()

                @pl.when(has_left)
                def _():
                    z_copy(c, i + s, 1).start()

    def z_drain(c):
        for block in range(n_col):
            @pl.when(has_right & (block <= i))
            def _():
                z_copy(c, block, 0).wait_send()

            @pl.when(has_left & (block >= i))
            def _():
                z_copy(c, block, 1).wait_send()

    def col_copy(m, block):
        return pltpu.make_async_remote_copy(
            src_ref=cols_near.at[block], dst_ref=cols_near.at[block],
            send_sem=c_send.at[m], recv_sem=c_recv.at[block // 2],
            device_id=row_dev(2 * flip(q, m) + core), device_id_type=MESH)

    def sib_copy(block):
        return pltpu.make_async_remote_copy(
            src_ref=cols_near.at[block], dst_ref=cols_near.at[block],
            send_sem=s_send.at[block // 2], recv_sem=s_recv.at[block // 2],
            device_id=row_dev(sib), device_id_type=MESH)

    def col_arrive(m):
        block = 2 * flip(q, m) + core
        col_copy(m, block).wait_recv()
        sib_copy(block).start()

    z_own(0)
    for m in reversed(range(1, chips)):
        col_copy(m, r).start()
    sib_copy(r).start()
    z_own(1)

    masks = list(range(1, chips))
    z_next = 0
    for at, m in enumerate(masks):
        if z_next < nc - 1 and at < nc - 1:
            z_forward(z_next)
            if z_next + 2 < nc:
                z_own(z_next + 2)
            z_next += 1
        col_arrive(m)
    for chip in range(chips):
        sib_copy(2 * chip + 1 - core).wait_recv()

    def row_copy(c, j, way, slot):
        return pltpu.make_async_remote_copy(
            src_ref=row_send[c].at[j], dst_ref=row_recv[c].at[slot],
            send_sem=rs_send.at[c, j], recv_sem=rs_recv.at[c, slot],
            device_id=col_dev(i + 1 - 2 * way), device_id_type=MESH)

    def row_pass(c):
        for s in range(1, n_col):
            far = n_col - s

            @pl.when(i - far >= 0)
            def _():
                j = i - far

                @pl.when(has_right)
                def _():
                    row_copy(c, j, 1, j).wait_recv()
                    row_send[c][j] = row_send[c][j] + row_recv[c][j]

                row_copy(c, j, 1, n_col if far == 1 else j).start()

            @pl.when(i + far < n_col)
            def _():
                j = i + far

                @pl.when(has_left)
                def _():
                    row_copy(c, j, 0, j).wait_recv()
                    row_send[c][j] = row_send[c][j] + row_recv[c][j]

                row_copy(c, j, 0, j).start()

    def row_finish(c):
        span = slice(c * width, (c + 1) * width)
        row_out[:, span] = row_send[c][i].astype(jnp.float32)

        @pl.when(has_left)
        def _():
            row_copy(c, i, 0, i).wait_recv()
            row_out[:, span] += row_recv[c][i].astype(jnp.float32)

        @pl.when(has_right)
        def _():
            row_copy(c, i, 1, n_col).wait_recv()
            row_out[:, span] += row_recv[c][n_col].astype(jnp.float32)

        for j in range(n_col):
            @pl.when(j != i)
            def _():
                row_copy(c, j, 0, j).wait_send()

    def compute(c):
        def one_tile(t, carry):
            piece = c * tiles + t
            row_block = rows_near[c][row_slots[t]]
            col_block = cols_near[col_slots[t]]
            count_copy(piece).wait()
            raw = count_buf[piece % count_slots]

            scores = lax.dot_general(
                row_block, col_block, (((0,), (0,)), ((), ())), preferred_element_type=jnp.float32)
            counted = jnp.maximum(raw, 1).astype(jnp.float32)
            residue = scores - jnp.log(counted)
            weighted = (0.1 * err_scale + 0.25 * err_scale * (counted * lax.rsqrt(counted))) * residue
            soft = 0.5 * err_scale * jnp.tanh(0.5 * residue) + 0.5 * err_scale
            errors = jnp.where(raw > 0, weighted, soft).astype(jnp.bfloat16)
            row_term[t] = lax.dot_general(
                col_block, errors, (((1,), (1,)), ((), ())), preferred_element_type=jnp.float32)
            grown = jnp.dot(row_block, errors, preferred_element_type=jnp.float32)
            if c == 0:
                col_term[t] = grown
            else:
                col_term[t] += grown

            @pl.when(piece + count_slots < nc * tiles)
            def _():
                count_copy(piece + count_slots).start()

            return carry

        lax.fori_loop(0, tiles, one_tile, 0)

        def one_dest(j, carry):
            total = row_term[0] * row_pick[j]
            for t in range(1, tiles):
                total += row_term[t] * row_pick[t * n_col + j]
            row_send[c][j] = total.astype(jnp.bfloat16)
            return carry

        lax.fori_loop(0, n_col, one_dest, 0)

    for c in range(nc):
        if c == z_next:
            z_forward(c)
            z_next += 1
            if c + 2 < nc:
                z_own(c + 2)
        compute(c)
        if z_next < nc and z_next == c + 1:
            z_forward(z_next)
            if z_next + 2 < nc:
                z_own(z_next + 2)
            z_next += 1
        if c > 0:
            row_pass(c - 1)

    def col_total(d):
        total = col_term[0] * col_pick[d]
        for t in range(1, tiles):
            total += col_term[t] * col_pick[t * n_row + d]
        return total.astype(jnp.bfloat16)

    def sib_sum(chip):
        return pltpu.make_async_remote_copy(
            src_ref=col_part.at[2 * chip + 1 - core], dst_ref=sib_recv.at[chip],
            send_sem=q_send.at[chip], recv_sem=q_recv.at[chip],
            device_id=row_dev(sib), device_id_type=MESH)

    def peer_sum(m):
        chip = flip(q, m)
        return pltpu.make_async_remote_copy(
            src_ref=col_part.at[2 * chip + core], dst_ref=peer_recv.at[m],
            send_sem=p_send.at[m], recv_sem=p_recv.at[m],
            device_id=row_dev(2 * chip + core), device_id_type=MESH)

    order = list(reversed(range(1, chips))) + [0]
    for m in order:
        chip = flip(q, m)
        col_part[2 * chip + 1 - core] = col_total(2 * chip + 1 - core)
        sib_sum(chip).start()
    row_pass(nc - 1)
    for m in order:
        chip = flip(q, m)
        mine = 2 * chip + core
        col_part[mine] = col_total(mine)
        sib_sum(chip).wait_recv()
        if m > 0:
            col_part[mine] = col_part[mine] + sib_recv[chip]
            peer_sum(m).start()
    col_out[...] = col_part[r].astype(jnp.float32) + sib_recv[q].astype(jnp.float32)

    for c in range(nc):
        row_finish(c)
    for m in range(1, chips):
        peer_sum(m).wait_recv()
        col_out[...] += peer_recv[m].astype(jnp.float32)

    for c in range(nc):
        z_drain(c)
    for m in range(1, chips):
        col_copy(m, r).wait_send()
        peer_sum(m).wait_send()
    for chip in range(chips):
        sib_copy(2 * chip + core).wait_send()
        sib_sum(chip).wait_send()


def adagrad(weights, history, gradient):
    grown = history + gradient * gradient
    return (weights - learn_rate * gradient / jnp.sqrt(grown), grown)


def body(row_emb, col_emb, row_acc, col_acc, marginal_log, tile_rows, tile_cols, counts):
    n_col = lax.axis_size("col")
    n_row = lax.axis_size("row")
    emb_width, block_len = row_emb.shape[1:]
    tiles = counts.shape[0]
    chips = n_row // 2
    nc = chunk_count
    width = block_len // nc
    me = lax.axis_index("row") * n_col + lax.axis_index("col")
    margin = lax.dynamic_slice_in_dim(marginal_log, me * block_len, block_len)
    high = lax.reduce_precision(margin, 8, 7)
    pair = jnp.stack([high, margin - high]).astype(jnp.bfloat16)
    padded = -(-(emb_width + 4) // 16) * 16
    ones = jnp.ones((2, block_len), jnp.bfloat16)
    zeros = jnp.zeros((padded - emb_width - 4, block_len), jnp.bfloat16)
    row_in = jnp.concatenate([row_emb[0].astype(jnp.bfloat16), pair, ones, zeros])
    col_in = jnp.concatenate([col_emb[0].astype(jnp.bfloat16), ones, pair, zeros])
    row_slots = tile_rows % n_col
    col_slots = tile_cols // n_col
    row_pick = (row_slots[:, None] == jnp.arange(n_col)[None, :]).astype(jnp.float32).reshape(-1)
    col_pick = (col_slots[:, None] == jnp.arange(n_row)[None, :]).astype(jnp.float32).reshape(-1)

    smem = pl.BlockSpec(memory_space=pltpu.SMEM)
    vmem = pl.BlockSpec(memory_space=pltpu.VMEM)
    bf16 = jnp.bfloat16
    dma = pltpu.SemaphoreType.DMA
    scratch = (
        [pltpu.VMEM((n_col, padded, width), bf16)] * nc
        + [pltpu.VMEM((n_col, padded, width), bf16)] * nc
        + [pltpu.VMEM((n_col + 1, padded, width), bf16)] * nc
        + [
            pltpu.VMEM((n_row, padded, block_len), bf16),
            pltpu.VMEM((n_row, padded, block_len), bf16),
            pltpu.VMEM((chips, padded, block_len), bf16),
            pltpu.VMEM((chips, padded, block_len), bf16),
            pltpu.VMEM((count_slots, width, block_len), jnp.int32),
            pltpu.VMEM((tiles, padded, width), jnp.float32),
            pltpu.VMEM((tiles, padded, block_len), jnp.float32),
            dma((2, nc, n_col)), dma((nc, n_col)),
            dma((chips,)), dma((chips,)), dma((chips,)), dma((chips,)),
            dma((count_slots,)),
            dma((nc, n_col)), dma((nc, n_col + 1)),
            dma((chips,)), dma((chips,)), dma((chips,)), dma((chips,)),
        ]
    )
    row_sum, col_sum = pl.pallas_call(
        functools.partial(step_kernel, n_row, n_col, tiles),
        out_shape=[jax.ShapeDtypeStruct((padded, block_len), jnp.float32)] * 2,
        in_specs=[smem] * 4 + [vmem] * 2 + [pl.BlockSpec(memory_space=pl.ANY)],
        out_specs=[vmem] * 2,
        scratch_shapes=scratch,
        compiler_params=pltpu.CompilerParams(
            collective_id=0, has_side_effects=True, vmem_limit_bytes=62 * 1024 * 1024),
    )(row_slots, col_slots, row_pick, col_pick, row_in, col_in, counts)
    new_row_emb, new_row_acc = adagrad(row_emb, row_acc, row_sum[None, :emb_width])
    new_col_emb, new_col_acc = adagrad(col_emb, col_acc, col_sum[None, :emb_width])
    return (new_row_emb, new_col_emb, new_row_acc, new_col_acc)


def solution(mesh):
    blocks = P(("row", "col"), None, None)
    listed = P(("row", "col"))
    return jax.shard_map(
        body,
        mesh=mesh,
        in_specs=(blocks, blocks, blocks, blocks, P(), listed, listed, blocks),
        out_specs=(blocks, blocks, blocks, blocks),
        check_vma=False,
    )
```

time: 257 us -> 162 us (0.63)
  waiting for transfers between devices: 166 us -> 0 us
  Pallas kernels: 0 us -> 143 us
  between operations: 31.4 us -> 0.72 us
  matrix products: 23.3 us -> 0 us
  local copies, waits for them, and re-layouts: 24.4 us -> 12.6 us
  other arithmetic: 8.85 us -> 5.81 us
    pallas_call x0 -> x1, Pallas kernels: none -> 143 us  [body(): pl.pallas_call(functools.partial(step_kernel, n_row, n_col, tiles), out_s...]
    reduce_scatter x2 -> x0, waiting for transfers between devices: 92.1 us -> none  [the longest x1 53.7 us: body(): lax.psum_scatter(grads[1].astype(jnp.bfloat16), 'row', scatter_dimension=...]
    all_gather x2 -> x0, waiting for transfers between devices: 74.3 us -> none  [the longest x1 43.6 us: body(): cols_near = lax.all_gather(col_low, 'row', axis=0, tiled=True)]
    dot_general x9 -> x0, matrix products: 23.3 us -> none  [the longest x3 18.2 us: tile_terms(): lax.dot_general(row_block, col_block, (((0,), (0,)), ((), ())), preferred...]
    unnamed x30 -> x16, local copies, waits for them, and re-layouts: 20.1 us -> 9.2 us
    convert_element_type x2, other arithmetic: 4.93 us -> 0.14 us  [the longest x1 0.07 us: body(): (col_slots[:, None] == jnp.arange(n_row)[None, :]).astype(jnp.float32)]
    convert_element_type x0 -> x3, local copies, waits for them, and re-layouts: none -> 3.36 us  [the longest x1 2.02 us: body(): col_emb[0].astype(jnp.bfloat16)]
  transfers between devices with their start and end apart: 4 -> 0, of which waited for: 4 -> 0; matrix products, arithmetic and copies ran while one was open for 7% -> 0% of each run, Pallas kernels for 0% -> 0%
where the time goes in v1:
time: 162 us
  Pallas kernels  143 us (88%)
  local copies, waits for them, and re-layouts  12.6 us (8%)
  other arithmetic  5.81 us (4%)
    pallas_call x1, Pallas kernels, body(): pl.pallas_call(functools.partial(step_kernel, n_row, n_col, tiles), out_s...  143 us
    unnamed x16, local copies, waits for them, and re-layouts  9.2 us

profile of v1, /device:TPU:9, one launch (start us, length us, event | category | flops | bytes accessed | tf_op | source)
XLA Modules:
  0.0 161.9 jit_solution(15061703606238179013)
XLA Ops:
  0.6 0.7 and_select_fusion
  1.3 0.0 copy-start.4
  1.3 0.0 copy-start.5
  1.3 0.1 fusion.6
  1.4 0.7 reshape.29.col_pick
  2.1 0.1 fusion.5
  2.1 0.7 reshape.28.row_pick
  2.8 0.7 reduce-precision_convert_fusion
  3.5 2.0 %fusion.2 = (bf16[300,1024]{1,0:T(8,128)(2,1)S(1)}, bf16[300,1024]{1,0:T(8,128)(2,1)S(1)}) fusion(f32[1,300,1024]{2,0,1:T(1,128)} %param.9, f32[1,300,1024]{2,0,1:T(1,128)} %param.8), kind=kLoop, calls=%fused_computation.8 | loop fusion | bytes 3686400 | tf_op jit(solution)/shard_map/convert_element_type | solution.py:336
  5.5 0.0 copy-done.4
  5.6 0.0 copy-done.5
  5.6 1.2 pad_maximum_fusion.1
  6.8 0.0 copy-start
  6.8 142.8 %shard_map.111 = (f32[304,1024]{1,0:T(8,128)}, f32[304,1024]{1,0:T(8,128)}) custom-call(s32[3]{0:T(128)} %copy-done.5, s32[3]{0:T(128)} %copy-done.4, f32[12]{0:T(128)} %reshape.28.row_pick, f32[24]{0:T(128)} %reshape.29.col_pick, bf16[304,1024]{1,0:T(8,128)(2,1)} %get-tuple-element.19.row_in, bf16[304,1024]{1,0:T(8,128)(2,1)} %get-tuple-element.18.col_in, ...), custom_call_target="tpu_custom_call" | custom-call | tf_op jit(solution)/shard_map/pallas_call | solution.py:365
  149.6 0.0 copy-done
  149.6 2.4 %fusion.1 = (f32[1,300,1024]{2,1,0:T(8,128)S(1)}, f32[1,300,1024]{2,1,0:T(8,128)S(1)}) fusion(f32[1,300,1024]{2,0,1:T(1,128)S(1)} %copy-done, f32[304,1024]{1,0:T(8,128)} %get-tuple-element.6, f32[1,300,1024]{2,0,1:T(1,128)} %param.10), kind=kLoop, calls=%fused_computation.5 | loop fusion | flops 1536000 | bytes 6144000 | tf_op jit(solution)/shard_map/sub | solution.py:317
  152.0 0.0 copy-start.3
  152.0 2.3 %copy.18 = f32[1,300,1024]{2,0,1:T(1,128)} copy(f32[1,300,1024]{2,1,0:T(8,128)S(1)} %get-tuple-element.14) | data formatting | bytes 2457600
  154.3 0.0 copy-start.1
  154.3 0.0 copy-start.2
  154.3 2.3 %copy.20 = f32[1,300,1024]{2,0,1:T(1,128)} copy(f32[1,300,1024]{2,1,0:T(8,128)S(1)} %get-tuple-element.15) | data formatting | bytes 2457600
  156.6 0.0 copy-done.3
  156.6 0.0 copy-done.1
  156.6 0.0 copy-done.2
  156.6 0.7 fusion
  157.3 2.3 %copy.19 = f32[1,300,1024]{2,0,1:T(1,128)} copy(f32[1,300,1024]{2,1,0:T(8,128)S(1)} %get-tuple-element.12) | data formatting | bytes 2457600
  159.6 2.3 %copy.21 = f32[1,300,1024]{2,0,1:T(1,128)} copy(f32[1,300,1024]{2,1,0:T(8,128)S(1)} %get-tuple-element.13) | data formatting | bytes 2457600
  (3 shorter events, 0.0 us)
Async XLA Ops:
  1.3 4.2 %copy-start.4 = (s32[3]{0:T(128)}, s32[3]{0:T(128)S(1)}, u32[]{:S(2)}) copy-start(s32[3]{0:T(128)S(1)} %get-tuple-element.22.col_slots) | copy-start | bytes 40
  1.3 4.2 %copy-start.5 = (s32[3]{0:T(128)}, s32[3]{0:T(128)S(1)}, u32[]{:S(2)}) copy-start(s32[3]{0:T(128)S(1)} %get-tuple-element.23.row_slots) | copy-start | bytes 40
  6.8 142.8 %copy-start = (f32[1,300,1024]{2,0,1:T(1,128)S(1)}, f32[1,300,1024]{2,0,1:T(1,128)}, u32[]{:S(2)}) copy-start(f32[1,300,1024]{2,0,1:T(1,128)} %param.8) | copy-start | bytes 3686404
  152.0 4.6 %copy-start.3 = (f32[1,300,1024]{2,0,1:T(1,128)S(1)}, f32[1,300,1024]{2,0,1:T(1,128)}, u32[]{:S(2)}) copy-start(f32[1,300,1024]{2,0,1:T(1,128)} %param.11) | copy-start | bytes 3686404
  154.3 2.3 %copy-start.1 = (f32[1,300,1024]{2,0,1:T(1,128)S(1)}, f32[1,300,1024]{2,0,1:T(1,128)}, u32[]{:S(2)}) copy-start(f32[1,300,1024]{2,0,1:T(1,128)} %param.9) | copy-start | bytes 3686404
  154.3 2.3 %copy-start.2 = (f32[304,1024]{1,0:T(8,128)S(1)}, f32[304,1024]{1,0:T(8,128)}, u32[]{:S(2)}) copy-start(f32[304,1024]{1,0:T(8,128)} %get-tuple-element.7) | copy-start | bytes 3735556

commit v2 on v1

--- a/solution.py
+++ b/solution.py
@@ -23,7 +23,7 @@
     return index
 
 
-def step_kernel(n_row, n_col, tiles, row_slots, col_slots, row_pick, col_pick, row_in, col_in,
+def step_kernel(n_row, n_col, tiles, tile_rows, tile_cols, row_in, col_in,
                 counts, row_out, col_out, *scratch):
     nc = chunk_count
     rows_near = scratch[:nc]
@@ -35,6 +35,7 @@
     chips = n_row // 2
     block_len = row_in.shape[1]
     width = block_len // nc
+    half = -(-row_in.shape[0] // 32) * 16
     r = lax.axis_index("row")
     i = lax.axis_index("col")
     q = r // 2
@@ -209,8 +210,8 @@
     def compute(c):
         def one_tile(t, carry):
             piece = c * tiles + t
-            row_block = rows_near[c][row_slots[t]]
-            col_block = cols_near[col_slots[t]]
+            row_block = rows_near[c][tile_rows[t] % n_col]
+            col_block = cols_near[tile_cols[t] // n_col]
             count_copy(piece).wait()
             raw = count_buf[piece % count_slots]
 
@@ -238,9 +239,9 @@
         lax.fori_loop(0, tiles, one_tile, 0)
 
         def one_dest(j, carry):
-            total = row_term[0] * row_pick[j]
+            total = jnp.where(tile_rows[0] % n_col == j, row_term[0], 0.0)
             for t in range(1, tiles):
-                total += row_term[t] * row_pick[t * n_col + j]
+                total += jnp.where(tile_rows[t] % n_col == j, row_term[t], 0.0)
             row_send[c][j] = total.astype(jnp.bfloat16)
             return carry
 
@@ -262,9 +263,9 @@
             row_pass(c - 1)
 
     def col_total(d):
-        total = col_term[0] * col_pick[d]
+        total = jnp.where(tile_cols[0] // n_col == d, col_term[0], 0.0)
         for t in range(1, tiles):
-            total += col_term[t] * col_pick[t * n_row + d]
+            total += jnp.where(tile_cols[t] // n_col == d, col_term[t], 0.0)
         return total.astype(jnp.bfloat16)
 
     def sib_sum(chip):
@@ -285,20 +286,51 @@
         chip = flip(q, m)
         col_part[2 * chip + 1 - core] = col_total(2 * chip + 1 - core)
         sib_sum(chip).start()
-    row_pass(nc - 1)
-    for m in order:
+
+    def col_own(m):
         chip = flip(q, m)
         mine = 2 * chip + core
-        col_part[mine] = col_total(mine)
+        total = col_total(mine)
         sib_sum(chip).wait_recv()
         if m > 0:
-            col_part[mine] = col_part[mine] + sib_recv[chip]
+            total = total + sib_recv[chip]
+        col_part[mine] = total
+
+    if chips == 4:
+        diag = 2 * flip(q, 3) + core
+        near_x, near_y = 2 * flip(q, 1) + core, 2 * flip(q, 2) + core
+
+        def half_sum(span, m, sem):
+            return pltpu.make_async_remote_copy(
+                src_ref=col_part.at[diag, span], dst_ref=peer_recv.at[0, span],
+                send_sem=p_send.at[sem], recv_sem=p_recv.at[sem],
+                device_id=row_dev(2 * flip(q, m) + core), device_id_type=MESH)
+
+        low, high = pl.ds(0, half), pl.ds(half, col_in.shape[0] - half)
+        col_own(3)
+        half_sum(low, 1, 0).start()
+        half_sum(high, 2, 3).start()
+        col_own(1)
+        col_own(2)
+        half_sum(high, 2, 3).wait_recv()
+        col_part[near_x, high] = col_part[near_x, high] + peer_recv[0, high]
+        peer_sum(1).start()
+        half_sum(low, 1, 0).wait_recv()
+        col_part[near_y, low] = col_part[near_y, low] + peer_recv[0, low]
+        peer_sum(2).start()
+        last = [1, 2]
+    else:
+        for m in order[:-1]:
+            col_own(m)
             peer_sum(m).start()
+        last = list(range(1, chips))
+    row_pass(nc - 1)
+    col_own(0)
     col_out[...] = col_part[r].astype(jnp.float32) + sib_recv[q].astype(jnp.float32)
 
     for c in range(nc):
         row_finish(c)
-    for m in range(1, chips):
+    for m in last:
         peer_sum(m).wait_recv()
         col_out[...] += peer_recv[m].astype(jnp.float32)
 
@@ -306,7 +338,11 @@
         z_drain(c)
     for m in range(1, chips):
         col_copy(m, r).wait_send()
+    for m in last:
         peer_sum(m).wait_send()
+    if chips == 4:
+        half_sum(low, 1, 0).wait_send()
+        half_sum(high, 2, 3).wait_send()
     for chip in range(chips):
         sib_copy(2 * chip + core).wait_send()
         sib_sum(chip).wait_send()
@@ -334,11 +370,6 @@
     zeros = jnp.zeros((padded - emb_width - 4, block_len), jnp.bfloat16)
     row_in = jnp.concatenate([row_emb[0].astype(jnp.bfloat16), pair, ones, zeros])
     col_in = jnp.concatenate([col_emb[0].astype(jnp.bfloat16), ones, pair, zeros])
-    row_slots = tile_rows % n_col
-    col_slots = tile_cols // n_col
-    row_pick = (row_slots[:, None] == jnp.arange(n_col)[None, :]).astype(jnp.float32).reshape(-1)
-    col_pick = (col_slots[:, None] == jnp.arange(n_row)[None, :]).astype(jnp.float32).reshape(-1)
-
     smem = pl.BlockSpec(memory_space=pltpu.SMEM)
     vmem = pl.BlockSpec(memory_space=pltpu.VMEM)
     bf16 = jnp.bfloat16
@@ -365,15 +396,19 @@
     row_sum, col_sum = pl.pallas_call(
         functools.partial(step_kernel, n_row, n_col, tiles),
         out_shape=[jax.ShapeDtypeStruct((padded, block_len), jnp.float32)] * 2,
-        in_specs=[smem] * 4 + [vmem] * 2 + [pl.BlockSpec(memory_space=pl.ANY)],
+        in_specs=[smem] * 2 + [vmem] * 2 + [pl.BlockSpec(memory_space=pl.ANY)],
         out_specs=[vmem] * 2,
         scratch_shapes=scratch,
         compiler_params=pltpu.CompilerParams(
             collective_id=0, has_side_effects=True, vmem_limit_bytes=62 * 1024 * 1024),
-    )(row_slots, col_slots, row_pick, col_pick, row_in, col_in, counts)
-    new_row_emb, new_row_acc = adagrad(row_emb, row_acc, row_sum[None, :emb_width])
-    new_col_emb, new_col_acc = adagrad(col_emb, col_acc, col_sum[None, :emb_width])
-    return (new_row_emb, new_col_emb, new_row_acc, new_col_acc)
+    )(tile_rows, tile_cols, row_in, col_in, counts)
+    def flat(block):
+        return lax.optimization_barrier(block.reshape(-1, 128))
+
+    rows = adagrad(flat(row_emb), flat(row_acc), flat(row_sum[:emb_width]))
+    cols = adagrad(flat(col_emb), flat(col_acc), flat(col_sum[:emb_width]))
+    ordered = lax.optimization_barrier((rows[0], cols[0], rows[1], cols[1]))
+    return tuple(out.reshape(row_emb.shape) for out in ordered)
 
 
 def solution(mesh):

time: 162 us -> 143 us (0.88)
  Pallas kernels: 143 us -> 128 us
  local copies, waits for them, and re-layouts: 12.6 us -> 6.03 us
    pallas_call x1, Pallas kernels: 143 us -> 128 us  [body(): pl.pallas_call(functools.partial(step_kernel, n_row, n_col, tiles), out_s...]
    unnamed x16 -> x6, local copies, waits for them, and re-layouts: 9.2 us -> 0.01 us
    reshape x0 -> x2, local copies, waits for them, and re-layouts: none -> 3.98 us  [flat(): return lax.optimization_barrier(block.reshape(-1, 128))]
    sub x2, other arithmetic: 3.13 us -> 5.19 us  [adagrad(): return (weights - learn_rate * gradient / jnp.sqrt(grown), grown)]
    convert_element_type x3 -> x1, local copies, waits for them, and re-layouts: 3.36 us -> 2.02 us  [body(): row_emb[0].astype(jnp.bfloat16)]
where the time goes in v2:
time: 143 us; the launch traced here: 142 us
  Pallas kernels  128 us (90%)
  other arithmetic  7.06 us (5%)
  local copies, waits for them, and re-layouts  6.03 us (4%)
    pallas_call x1, Pallas kernels, body(): pl.pallas_call(functools.partial(step_kernel, n_row, n_col, tiles), out_s...  128 us
    sub x2, other arithmetic, adagrad(): return (weights - learn_rate * gradient / jnp.sqrt(grown), grown)  5.19 us
    reshape x2, local copies, waits for them, and re-layouts, flat(): return lax.optimization_barrier(block.reshape(-1, 128))  3.98 us

profile of v2, /device:TPU:9, one launch (start us, length us, event | category | flops | bytes accessed | tf_op | source)
XLA Modules:
  0.0 142.1 jit_solution(4540566004440705115)
XLA Ops:
  0.6 0.7 reduce-precision_convert_fusion
  1.3 2.0 %fusion = (bf16[300,1024]{1,0:T(8,128)(2,1)S(1)}, bf16[300,1024]{1,0:T(8,128)(2,1)S(1)}) fusion(f32[1,300,1024]{2,0,1:T(1,128)} %param.8, f32[1,300,1024]{2,0,1:T(1,128)} %param.9), kind=kLoop, calls=%fused_computation.6 | loop fusion | bytes 3686400 | tf_op jit(solution)/shard_map/convert_element_type | solution.py:371
  3.4 1.2 pad_maximum_fusion.1
  4.6 128.4 %shard_map.111 = (f32[304,1024]{1,0:T(8,128)}, f32[304,1024]{1,0:T(8,128)}) custom-call(s32[3]{0:T(128)} %tile_rows.1, s32[3]{0:T(128)} %tile_cols.1, bf16[304,1024]{1,0:T(8,128)(2,1)} %get-tuple-element.23.row_in, bf16[304,1024]{1,0:T(8,128)(2,1)} %get-tuple-element.22.col_in, s32[3,1024,1024]{2,1,0:T(8,128)} %counts.1), custom_call_target="tpu_custom_call" | custom-call | tf_op jit(solution)/shard_map/pallas_call | solution.py:396
  132.9 1.5 %reshape.41 = f32[2400,128]{1,0:T(8,128)S(1)} reshape(f32[300,1024]{1,0:T(8,128)} %bitcast.17) | data formatting | bytes 2457600 | tf_op jit(solution)/shard_map/reshape | solution.py:406
  134.4 0.0 copy-start
  134.4 2.5 %reshape.44 = f32[2400,128]{1,0:T(8,128)} reshape(f32[300,1024]{1,0:T(8,128)} %bitcast.16) | data formatting | bytes 2457600 | tf_op jit(solution)/shard_map/reshape | solution.py:406
  136.9 0.0 copy-done
  136.9 0.0 copy-start.1
  136.9 0.0 copy-start.2
  136.9 3.5 %multiply_subtract_fusion = (f32[2400,128]{1,0:T(8,128)}, f32[2400,128]{1,0:T(8,128)}) fusion(f32[2400,128]{1,0:T(8,128)S(1)} %bitcast.14, f32[2400,128]{1,0:T(8,128)} %reshape.44, f32[2400,128]{1,0:T(8,128)} %bitcast.18), kind=kLoop, calls=%fused_computation.2 | loop fusion | flops 1536000 | bytes 6144000 | tf_op jit(solution)/shard_map/sub | solution.py:353
  140.4 0.0 copy-done.1
  140.4 0.0 copy-done.2
  140.4 1.7 %multiply_subtract_fusion.1 = (f32[2400,128]{1,0:T(8,128)}, f32[2400,128]{1,0:T(8,128)}) fusion(f32[2400,128]{1,0:T(8,128)S(1)} %bitcast.15, f32[2400,128]{1,0:T(8,128)S(1)} %reshape.41, f32[2400,128]{1,0:T(8,128)S(1)} %bitcast.19), kind=kLoop, calls=%fused_computation.4 | loop fusion | flops 1536000 | bytes 6144000 | tf_op jit(solution)/shard_map/sub | solution.py:353
  (3 shorter events, 0.0 us)
Async XLA Ops:
  134.4 2.5 %copy-start = (f32[1,300,1024]{2,0,1:T(1,128)S(1)}, f32[1,300,1024]{2,0,1:T(1,128)}, u32[]{:S(2)}) copy-start(f32[1,300,1024]{2,0,1:T(1,128)} %param.9) | copy-start | bytes 3686404
  136.9 3.5 %copy-start.1 = (f32[1,300,1024]{2,0,1:T(1,128)S(1)}, f32[1,300,1024]{2,0,1:T(1,128)}, u32[]{:S(2)}) copy-start(f32[1,300,1024]{2,0,1:T(1,128)} %param.8) | copy-start | bytes 3686404
  136.9 3.5 %copy-start.2 = (f32[1,300,1024]{2,0,1:T(1,128)S(1)}, f32[1,300,1024]{2,0,1:T(1,128)}, u32[]{:S(2)}) copy-start(f32[1,300,1024]{2,0,1:T(1,128)} %param.10) | copy-start | bytes 3686404
